TPU v7x, 128 devices: a whole 4x4x4 slice. The times are simulated.
128 devices in a mesh: dp: 4 (over z), seq: 4 (over y), tensor: 8 (over x, core).
Axes of the slice: x: 4, y: 4, z: 4, core: 2. Of those that a mesh axis runs over, the one named last changes fastest.
Arguments:
- activations: bfloat16 [12, 352, 8192], P('dp', 'seq', 'tensor'), may hold values from -6 to 6
- cotangents: bfloat16 [12, 352, 14336], P('dp', 'seq', 'tensor'), may hold values from -0.59765625 to 0.59765625
- row_ids: int32 [4, 3], P('dp'), may hold values from 0 to 2, each once within a row
- row_counts: int32 [4, 3], P('dp'), may hold values from 88 to 352
Outputs:
- weighted_grad: float32 [8192, 14336], P(('dp', 'seq'), 'tensor')
- example_weights: float32 [4, 2], P('dp')
All inputs are finite; a program needn't handle non-finite values.
Results may differ from a plain program's by a relative error of at most 0.004.
Values may be sent and summed in bfloat16 or wider, within the bound.
A program may use at most 128 MiB of HBM per device.

v0:
```python
import jax
import jax.numpy as jnp
from jax import lax
from jax.experimental import pallas as pl
from jax.experimental.pallas import tpu as pltpu
from jax.sharding import PartitionSpec as P

MESH = pl.DeviceIdType.MESH
F32 = jnp.float32
BF16 = jnp.bfloat16

SEG = 88
NOISE = 176
CLEAN_ROWS = 96
WA = 768
WB = 1024
LANES = 128


def body_kernel(ids_ref, counts_ref, acts_ref, cot_ref, out_ref, wout_ref,
                na, ca, cg, ga, gb, ao, ata, atb, acc, gr, d2, sm, x3,
                sv1, sv2, sv3, wts, scale,
                ring_s, ring_r, p_s, p_r, p_l, x_s, x_r, k_s, k_r,
                d_s, d_r, m_s, m_r, v_s, v_r, o_s):
    z = lax.axis_index("dp")
    y = lax.axis_index("seq")
    t = lax.axis_index("tensor")
    x = t // 2
    c = lax.rem(t, 2)

    def mod4(v):
        return lax.rem(v, 4)

    def copy(src, dst, s, r, dev):
        return pltpu.make_async_remote_copy(
            src_ref=src, dst_ref=dst, send_sem=s, recv_sem=r, device_id=dev, device_id_type=MESH)

    barrier = pltpu.get_barrier_semaphore()

    def greet(dev):
        pl.semaphore_signal(barrier, inc=1, device_id=dev, device_id_type=MESH)

    for r in range(1, 4):
        greet((mod4(z + r), y, t))
        greet((z, mod4(y + r), t))
    for r in range(1, 8):
        greet((z, y, lax.rem(t + r, 8)))

    targets = [(h, q, (x, 2 * c + h, 2 * q + z // 2)) for h in range(2) for q in range(4)]
    target_self = [(x == z) & (y == 2 * c + h) & (q == x) & (c == z // 2) for h, q, _ in targets]
    sources = [(2 * c + i // 4, i % 4) for i in range(8)]
    source_self = [(zs == z) & (ys == y) & (x == z) & (c == y // 2) for zs, ys in sources]
    for (_, _, dev), same in zip(targets, target_self):
        @pl.when(jnp.logical_not(same))
        def _():
            greet(dev)
    for (zs, ys), same in zip(sources, source_self):
        @pl.when(jnp.logical_not(same))
        def _():
            greet((zs, ys, 2 * z + y // 2))
    has_self = ((x == z) & (c == y // 2) & (c == z // 2)).astype(jnp.int32)

    rid = [ids_ref[0, j] for j in range(3)]
    live = [counts_ref[0, rid[j]] - y * SEG for j in range(3)]
    rows = lax.broadcasted_iota(jnp.int32, (SEG, LANES), 0)
    pad = jnp.zeros((CLEAN_ROWS - SEG, LANES), F32)

    def stage_acts(i, carry):
        cols = pl.ds(pl.multiple_of(i * LANES, LANES), LANES)
        part = [acts_ref[rid[j], :, cols].astype(F32) for j in range(3)]
        na[y, :, cols] = jnp.concatenate([part[1], part[2]], axis=0).astype(BF16)
        ca[z, :, cols] = jnp.concatenate([part[0], pad], axis=0).astype(BF16)
        return carry

    lax.fori_loop(0, 1024 // LANES, stage_acts, 0)

    def masked(j, cols):
        return jnp.where(rows < live[j], cot_ref[rid[j], :, cols].astype(F32), 0.0)

    pl.semaphore_wait(barrier, 29 - 2 * has_self)

    pieces = []
    for i, ((h, q, dev), same) in enumerate(zip(targets, target_self)):
        src = na.at[y, :, pl.ds(h * 512 + q * LANES, LANES)]
        dst = ao.at[q, z, y]
        far_copy = copy(src, dst, p_s.at[i], p_r.at[lax.rem(z, 2) * 4 + y], dev)
        near_copy = pltpu.make_async_copy(src, dst, p_l)

        @pl.when(same)
        def _():
            near_copy.start()

        @pl.when(jnp.logical_not(same))
        def _():
            far_copy.start()
        pieces.append((far_copy, near_copy, same))

    rings = []

    class Ring:
        def __init__(self, at, axis, width):
            n = len(rings)
            rings.append(self)
            me = y if axis == "y" else z

            def dev(v):
                return (z, v, t) if axis == "y" else (v, y, t)

            up, down, far = mod4(me + 1), mod4(me + 3), mod4(me + 2)
            half = width // 2
            first, second = pl.ds(0, half), pl.ds(half, half)
            own, low, high, opp = at(me), at(down), at(up), at(far)
            self.go = [copy(own, own, ring_s.at[n, 0], ring_r.at[n, 0], dev(up)),
                       copy(own, own, ring_s.at[n, 1], ring_r.at[n, 1], dev(down))]
            self.got = [copy(low, low, ring_s.at[n, 0], ring_r.at[n, 0], dev(up)),
                        copy(high, high, ring_s.at[n, 1], ring_r.at[n, 1], dev(down))]
            self.pass_on = [
                copy(low.at[:, first], low.at[:, first], ring_s.at[n, 2], ring_r.at[n, 2], dev(up)),
                copy(high.at[:, second], high.at[:, second], ring_s.at[n, 3], ring_r.at[n, 3], dev(down))]
            self.got_far = [
                copy(opp.at[:, first], opp.at[:, first], ring_s.at[n, 2], ring_r.at[n, 2], dev(up)),
                copy(opp.at[:, second], opp.at[:, second], ring_s.at[n, 3], ring_r.at[n, 3], dev(down))]

        def start(self):
            for k in self.go:
                k.start()

        def forward(self):
            for k in range(2):
                self.got[k].wait_recv()
                self.pass_on[k].start()

        def finish(self):
            for k in self.got_far:
                k.wait_recv()

        def drain(self):
            for k in self.go + self.pass_on:
                k.wait_send()

    def az_ring(k):
        item = mod4(y + k)
        return Ring(lambda v: ga.at[v, item], "z", WA)

    def by_ring(k):
        item = mod4(z + k)
        return Ring(lambda v: gb.at[v, item], "y", WB)

    r_na = Ring(lambda v: na.at[v], "y", 1024)
    r_ca = Ring(lambda v: ca.at[v], "z", 1024)
    r_cg = Ring(lambda v: cg.at[v], "z", WA + WB)
    r_ay = Ring(lambda v: ga.at[z, v], "y", WA)
    r_bz = Ring(lambda v: gb.at[y, v], "z", WB)
    r_az = {k: az_ring(k) for k in (0, 3, 1, 2)}
    r_by = {k: by_ring(k) for k in (0, 3, 1, 2)}

    r_na.start()
    r_ca.start()

    def stage_clean(i, carry):
        cols = pl.ds(pl.multiple_of(i * LANES, LANES), LANES)
        cg[z, :, cols] = jnp.concatenate([masked(0, cols), pad], axis=0).astype(BF16)
        return carry

    lax.fori_loop(0, (WA + WB) // LANES, stage_clean, 0)
    r_cg.start()

    def stage_a(i, carry):
        cols = pl.ds(pl.multiple_of(i * LANES, LANES), LANES)
        ga[z, y, :, cols] = jnp.concatenate([masked(1, cols), masked(2, cols)], axis=0).astype(BF16)
        return carry

    lax.fori_loop(0, WA // LANES, stage_a, 0)
    r_ay.start()

    def stage_b(i, carry):
        cols = pl.ds(pl.multiple_of(i * LANES, LANES), LANES)
        from_cols = pl.ds(pl.multiple_of(WA + i * LANES, LANES), LANES)
        gb[y, z, :, cols] = jnp.concatenate(
            [masked(1, from_cols), masked(2, from_cols)], axis=0).astype(BF16)
        return carry

    lax.fori_loop(0, WB // LANES, stage_b, 0)
    r_bz.start()
    r_by[0].start()
    r_az[0].start()

    r_na.forward()
    here = pl.ds(2 * c, 2)
    there = pl.ds(2 * (1 - c), 2)
    for i, ((zs, ys), same) in enumerate(zip(sources, source_self)):
        dst = ao.at[x, zs, ys]
        far_copy = copy(dst, dst, p_s.at[i], p_r.at[i], (z, y, lax.rem(t + 1, 8)))
        near_copy = pltpu.make_async_copy(dst, dst, p_l)

        @pl.when(same)
        def _():
            near_copy.wait()

        @pl.when(jnp.logical_not(same))
        def _():
            far_copy.wait_recv()
    mine = ao.at[x, here]
    partner = (z, y, 2 * x + 1 - c)
    spread = [copy(mine, mine, x_s.at[r - 1], x_r.at[r - 1], (z, y, 2 * mod4(x + r) + c)) for r in range(1, 4)]
    for k in spread:
        k.start()
    core = [copy(mine, mine, k_s.at[0], k_r.at[0], partner)]
    core[0].start()

    r_ca.forward()
    r_cg.forward()
    r_ay.forward()
    r_az[3].start()
    r_az[1].start()
    r_bz.forward()
    r_by[3].start()
    r_by[1].start()
    r_by[0].forward()
    r_az[0].forward()

    for r in range(1, 4):
        block = ao.at[mod4(x + 4 - r), here]
        copy(block, block, x_s.at[r - 1], x_r.at[r - 1], partner).wait_recv()
        relay = copy(block, block, k_s.at[r], k_r.at[r], partner)
        relay.start()
        core.append(relay)

    contract = (((1,), (1,)), ((), ()))

    def gram(left, right):
        return lax.dot_general(left, right, contract, preferred_element_type=F32)

    r_na.finish()
    r_ca.finish()
    gr[0] = gram(na[...].reshape(4 * NOISE, 1024), ca[...].reshape(4 * CLEAN_ROWS, 1024))
    r_cg.finish()
    r_ay.finish()
    r_az[2].start()
    r_bz.finish()
    r_by[2].start()
    r_by[0].finish()
    gr[1] = gram(ga[z].reshape(4 * NOISE, WA), cg[:, :, :WA].reshape(4 * CLEAN_ROWS, WA)) + gram(
        gb[:, z].reshape(4 * NOISE, WB), cg[:, :, WA:].reshape(4 * CLEAN_ROWS, WB))
    away = gr.at[:, pl.ds(pl.multiple_of((1 - c) * 352, 8), 352)]
    swap = copy(away, d2, d_s, d_r, partner)
    swap.start()

    for r in range(4):
        block = ao.at[mod4(x + 4 - r), there]
        copy(block, block, k_s.at[r], k_r.at[r], partner).wait_recv()

    def turn(k, carry):
        for q in range(4):
            span = pl.ds(q * LANES, LANES)
            ata[k, span, :] = ao[q, k].reshape(4 * NOISE, LANES).T
            atb[k, span, :] = ao[q, :, k].reshape(4 * NOISE, LANES).T
        return carry

    lax.fori_loop(0, 4, turn, 0)

    swap.wait_recv()
    sm[...] = gr[:, pl.ds(pl.multiple_of(c * 352, 8), 352)] + d2[...]
    share = []
    for r in range(1, 4):
        to = mod4(x + r)
        share.append(copy(sm.at[:, pl.ds(pl.multiple_of(to * SEG, 8), SEG)], x3.at[r - 1],
                          m_s.at[r - 1], m_r.at[r - 1], (z, y, 2 * to + c)))
    for k in share:
        k.start()

    for k in (3, 1):
        r_az[k].forward()
        r_by[k].forward()

    for k in share:
        k.wait_recv()
    total = sm[:, pl.ds(pl.multiple_of(x * SEG, 8), SEG)] + x3[0] + x3[1] + x3[2]
    dot = jnp.sum(jnp.sum(total[0] * total[1], axis=0, keepdims=True), axis=1, keepdims=True)
    slot = 2 * z + lax.rem(x, 2)
    place = lax.broadcasted_iota(jnp.int32, (8, LANES), 0)
    tile = jnp.where(place == slot, jnp.broadcast_to(dot, (8, LANES)), 0.0)

    sends = []

    def exchange(buf, value, me, n, dev, base):
        buf[me] = value
        out = [copy(buf.at[me], buf.at[me], v_s.at[base + r], v_r.at[base + r], dev(lax.rem(me + r, n)))
               for r in range(1, n)]
        for k in out:
            k.start()
        sends.extend(out)
        for r in range(1, n):
            origin = lax.rem(me + n - r, n)
            copy(buf.at[origin], buf.at[origin], v_s.at[base + r], v_r.at[base + r], dev(origin)).wait_recv()
        return jnp.sum(buf[...], axis=0)

    tile = exchange(sv1, tile, t, 8, lambda v: (z, y, v), 0)
    tile = exchange(sv2, tile, y, 4, lambda v: (z, v, t), 8)
    tile = exchange(sv3, tile, z, 4, lambda v: (v, y, t), 12)
    weights = jnp.maximum(-tile, 0.0) / jnp.sum(jnp.abs(tile), axis=0, keepdims=True)
    wts[...] = weights
    for k in range(4):
        scale[k, :SEG] = jnp.broadcast_to(wts[2 * k:2 * k + 1, :], (SEG, LANES))
        scale[k, SEG:] = jnp.broadcast_to(wts[2 * k + 1:2 * k + 2, :], (SEG, LANES))
    lane = lax.broadcasted_iota(jnp.int32, (1, LANES), 1)
    wout_ref[...] = jnp.where(lane == 0, wts[pl.ds(2 * z, 1), :], wts[pl.ds(2 * z + 1, 1), :])[:, :2]

    r_az[2].forward()
    r_by[2].forward()

    def scaled(raw, s):
        full = jnp.concatenate([s, s], axis=1)
        return (raw.astype(F32) * full).astype(BF16)

    def product(at, pieces_of, width, base, first):
        def step(i, carry):
            cols = pl.ds(pl.multiple_of(i * 256, 256), 256)
            dest = pl.ds(pl.multiple_of(base + i * 256, 256), 256)
            right = jnp.concatenate([scaled(raw, s) for raw, s in pieces_of(cols)], axis=0)
            value = jnp.dot(at[...], right, preferred_element_type=F32)
            if first:
                acc[:, dest] = value
            else:
                acc[:, dest] += value
            return carry

        lax.fori_loop(0, width // 256, step, 0)

    def add_a(k, first=False):
        v = mod4(z + k)
        product(ata.at[v], lambda cols: [(ga[v, i, :, cols], scale[v]) for i in range(4)], WA, 0, first)

    def add_b(k, first=False):
        v = mod4(y + k)
        product(atb.at[v], lambda cols: [(gb[v, i, :, cols], scale[i]) for i in range(4)], WB, WA, first)

    add_a(0, True)
    add_b(0, True)
    for k in (3, 1):
        add_a(k)
        add_b(k)
    for k in (0, 3, 1, 2):
        r_az[k].finish()
    add_a(2)
    out_a = pltpu.make_async_copy(acc.at[:, pl.ds(0, WA)], out_ref.at[:, pl.ds(0, WA)], o_s.at[0])
    out_a.start()
    for k in (3, 1, 2):
        r_by[k].finish()
    add_b(2)
    out_b = pltpu.make_async_copy(acc.at[:, pl.ds(WA, WB)], out_ref.at[:, pl.ds(WA, WB)], o_s.at[1])
    out_b.start()

    for far_copy, _, same in pieces:
        @pl.when(jnp.logical_not(same))
        def _():
            far_copy.wait_send()
    for ring in rings:
        ring.drain()
    for k in spread + core + [swap] + share + sends:
        k.wait_send()
    out_a.wait()
    out_b.wait()


def body(activations, cotangents, row_ids, row_counts):
    dma = pltpu.SemaphoreType.DMA
    vmem = pltpu.VMEM
    return pl.pallas_call(
        body_kernel,
        out_shape=(jax.ShapeDtypeStruct((512, WA + WB), F32), jax.ShapeDtypeStruct((1, 2), F32)),
        in_specs=[pl.BlockSpec(memory_space=pltpu.SMEM)] * 2 + [pl.BlockSpec(memory_space=pltpu.VMEM)] * 2,
        out_specs=(pl.BlockSpec(memory_space=pl.ANY), pl.BlockSpec(memory_space=pltpu.VMEM)),
        scratch_shapes=[
            vmem((4, NOISE, 1024), BF16),
            vmem((4, CLEAN_ROWS, 1024), BF16),
            vmem((4, CLEAN_ROWS, WA + WB), BF16),
            vmem((4, 4, NOISE, WA), BF16),
            vmem((4, 4, NOISE, WB), BF16),
            vmem((4, 4, 4, NOISE, LANES), BF16),
            vmem((4, 512, 4 * NOISE), BF16),
            vmem((4, 512, 4 * NOISE), BF16),
            vmem((512, WA + WB), F32),
            vmem((2, 4 * NOISE, 4 * CLEAN_ROWS), F32),
            vmem((2, 2 * NOISE, 4 * CLEAN_ROWS), F32),
            vmem((2, 2 * NOISE, 4 * CLEAN_ROWS), F32),
            vmem((3, 2, SEG, 4 * CLEAN_ROWS), F32),
            vmem((8, 8, LANES), F32),
            vmem((4, 8, LANES), F32),
            vmem((4, 8, LANES), F32),
            vmem((8, LANES), F32),
            vmem((4, NOISE, LANES), F32),
            dma((13, 4)), dma((13, 4)),
            dma((8,)), dma((8,)), dma,
            dma((3,)), dma((3,)),
            dma((4,)), dma((4,)),
            dma, dma,
            dma((3,)), dma((3,)),
            dma((16,)), dma((16,)),
            dma((2,)),
        ],
        compiler_params=pltpu.CompilerParams(
            collective_id=0, has_side_effects=True, vmem_limit_bytes=60 * 1024 * 1024),
        cost_estimate=pl.CostEstimate(flops=8_000_000_000, bytes_accessed=8_000_000, transcendentals=0),
        name="reweight",
    )(row_ids, row_counts, activations, cotangents)


def solution(mesh):
    placed = (P("dp", "seq", "tensor"), P("dp", "seq", "tensor"), P("dp", None), P("dp", None))
    return jax.shard_map(
        body,
        mesh=mesh,
        in_specs=placed,
        out_specs=(P(("dp", "seq"), "tensor"), P("dp", None)),
        check_vma=False,
    )
```

profile of v0, /device:TPU:0, one launch (start us, length us, event | category | flops | bytes accessed | tf_op | source)
XLA Modules:
  0.0 111.4 jit_solution(12998288371075417813)
XLA Ops:
  0.6 106.1 %reweight.1 = (f32[512,1792]{1,0:T(8,128)}, f32[1,2]{1,0:T(1,128)}) custom-call(s32[1,3]{1,0:T(1,128)} %ids_ref.1, s32[1,3]{1,0:T(1,128)} %counts_ref.1, bf16[3,88,1024]{2,1,0:T(8,128)(2,1)} %acts_ref.1, bf16[3,88,1792]{2,1,0:T(8,128)(2,1)} %cot_ref.1), custom_call_target="tpu_custom_call" | custom-call | flops 8000000000 | bytes 8000000 | tf_op jit(solution)/shard_map/reweight/pallas_call | solution.py:369
  106.8 0.0 copy-start
  106.8 4.1 %copy.8 = f32[512,1792]{1,0:T(8,128)} copy(f32[512,1792]{1,0:T(8,128)} %get-tuple-element.4) | data formatting | bytes 7340032
  110.9 0.0 copy-done
  110.9 0.5 copy.9
Async XLA Ops:
  106.8 4.1 %copy-start = (f32[1,2]{1,0:T(1,128)S(1)}, f32[1,2]{1,0:T(1,128)}, u32[]{:S(2)}) copy-start(f32[1,2]{1,0:T(1,128)} %get-tuple-element.5) | copy-start | bytes 28
where the time goes:
time: 112 us; the launch traced here: 111 us
  Pallas kernels  106 us (95%)
  local copies, waits for them, and re-layouts  4.63 us (4%)
    pallas_call x1, Pallas kernels, body(): pl.pallas_call(body_kernel, out_shape=(jax.ShapeDtypeStruct((512, WA + WB...  106 us
    unnamed x4, local copies, waits for them, and re-layouts  4.63 us

commit v1 on v0

--- a/solution.py
+++ b/solution.py
@@ -18,8 +18,8 @@
 
 
 def body_kernel(ids_ref, counts_ref, acts_ref, cot_ref, out_ref, wout_ref,
-                na, ca, cg, ga, gb, ao, ata, atb, acc, gr, d2, sm, x3,
-                sv1, sv2, sv3, wts, scale,
+                na, ca, cg, ga, gb, ao, ata, atb, acc, part_gram, grad_gram, full, d2, sm,
+                near_a, near_b, x3, sv1, sv2, wts, scale,
                 ring_s, ring_r, p_s, p_r, p_l, x_s, x_r, k_s, k_r,
                 d_s, d_r, m_s, m_r, v_s, v_r, o_s):
     z = lax.axis_index("dp")
@@ -40,9 +40,12 @@
     def greet(dev):
         pl.semaphore_signal(barrier, inc=1, device_id=dev, device_id_type=MESH)
 
-    for r in range(1, 4):
-        greet((mod4(z + r), y, t))
-        greet((z, mod4(y + r), t))
+    def cell(r):
+        other = lax.rem(4 * z + y + r, 16)
+        return other // 4, lax.rem(other, 4), t
+
+    for r in range(1, 16):
+        greet(cell(r))
     for r in range(1, 8):
         greet((z, y, lax.rem(t + r, 8)))
 
@@ -77,7 +80,27 @@
     def masked(j, cols):
         return jnp.where(rows < live[j], cot_ref[rid[j], :, cols].astype(F32), 0.0)
 
-    pl.semaphore_wait(barrier, 29 - 2 * has_self)
+    def stage_clean(i, carry):
+        cols = pl.ds(pl.multiple_of(i * LANES, LANES), LANES)
+        cg[z, :, cols] = jnp.concatenate([masked(0, cols), pad], axis=0).astype(BF16)
+        return carry
+
+    def stage_a(i, carry):
+        cols = pl.ds(pl.multiple_of(i * LANES, LANES), LANES)
+        ga[z, y, :, cols] = jnp.concatenate([masked(1, cols), masked(2, cols)], axis=0).astype(BF16)
+        return carry
+
+    def stage_b(i, carry):
+        cols = pl.ds(pl.multiple_of(i * LANES, LANES), LANES)
+        from_cols = pl.ds(pl.multiple_of(WA + i * LANES, LANES), LANES)
+        gb[y, z, :, cols] = jnp.concatenate(
+            [masked(1, from_cols), masked(2, from_cols)], axis=0).astype(BF16)
+        return carry
+
+    lax.fori_loop(0, WA // LANES, stage_a, 0)
+    lax.fori_loop(0, (WA + WB) // LANES, stage_clean, 0)
+    lax.fori_loop(0, WB // LANES, stage_b, 0)
+    pl.semaphore_wait(barrier, 38 - 2 * has_self)
 
     pieces = []
     for i, ((h, q, dev), same) in enumerate(zip(targets, target_self)):
@@ -98,28 +121,26 @@
     rings = []
 
     class Ring:
-        def __init__(self, at, axis, width):
+        def __init__(self, at, axis, first, second):
             n = len(rings)
             rings.append(self)
-            me = y if axis == "y" else z
+            me = {"x": x, "y": y, "z": z}[axis]
 
             def dev(v):
-                return (z, v, t) if axis == "y" else (v, y, t)
+                return {"x": (z, y, 2 * v + c), "y": (z, v, t), "z": (v, y, t)}[axis]
 
             up, down, far = mod4(me + 1), mod4(me + 3), mod4(me + 2)
-            half = width // 2
-            first, second = pl.ds(0, half), pl.ds(half, half)
             own, low, high, opp = at(me), at(down), at(up), at(far)
             self.go = [copy(own, own, ring_s.at[n, 0], ring_r.at[n, 0], dev(up)),
                        copy(own, own, ring_s.at[n, 1], ring_r.at[n, 1], dev(down))]
             self.got = [copy(low, low, ring_s.at[n, 0], ring_r.at[n, 0], dev(up)),
                         copy(high, high, ring_s.at[n, 1], ring_r.at[n, 1], dev(down))]
             self.pass_on = [
-                copy(low.at[:, first], low.at[:, first], ring_s.at[n, 2], ring_r.at[n, 2], dev(up)),
-                copy(high.at[:, second], high.at[:, second], ring_s.at[n, 3], ring_r.at[n, 3], dev(down))]
+                copy(low.at[first], low.at[first], ring_s.at[n, 2], ring_r.at[n, 2], dev(up)),
+                copy(high.at[second], high.at[second], ring_s.at[n, 3], ring_r.at[n, 3], dev(down))]
             self.got_far = [
-                copy(opp.at[:, first], opp.at[:, first], ring_s.at[n, 2], ring_r.at[n, 2], dev(up)),
-                copy(opp.at[:, second], opp.at[:, second], ring_s.at[n, 3], ring_r.at[n, 3], dev(down))]
+                copy(opp.at[first], opp.at[first], ring_s.at[n, 2], ring_r.at[n, 2], dev(up)),
+                copy(opp.at[second], opp.at[second], ring_s.at[n, 3], ring_r.at[n, 3], dev(down))]
 
         def start(self):
             for k in self.go:
@@ -138,54 +159,38 @@
             for k in self.go + self.pass_on:
                 k.wait_send()
 
+    def halves(width):
+        half = width // 2
+        return (slice(None), pl.ds(0, half)), (slice(None), pl.ds(half, half))
+
     def az_ring(k):
         item = mod4(y + k)
-        return Ring(lambda v: ga.at[v, item], "z", WA)
+        return Ring(lambda v: ga.at[v, item], "z", *halves(WA))
 
     def by_ring(k):
         item = mod4(z + k)
-        return Ring(lambda v: gb.at[v, item], "y", WB)
-
-    r_na = Ring(lambda v: na.at[v], "y", 1024)
-    r_ca = Ring(lambda v: ca.at[v], "z", 1024)
-    r_cg = Ring(lambda v: cg.at[v], "z", WA + WB)
-    r_ay = Ring(lambda v: ga.at[z, v], "y", WA)
-    r_bz = Ring(lambda v: gb.at[y, v], "z", WB)
+        return Ring(lambda v: gb.at[v, item], "y", *halves(WB))
+
+    def rows_of(chunk):
+        return pl.ds(pl.multiple_of(chunk * SEG, 8), SEG)
+
+    r_na = Ring(lambda v: na.at[v], "y", *halves(1024))
+    r_ca = Ring(lambda v: ca.at[v], "z", *halves(1024))
+    r_cg = Ring(lambda v: cg.at[v], "z", *halves(WA + WB))
+    r_ay = Ring(lambda v: ga.at[z, v], "y", *halves(WA))
+    r_bz = Ring(lambda v: gb.at[y, v], "z", *halves(WB))
     r_az = {k: az_ring(k) for k in (0, 3, 1, 2)}
     r_by = {k: by_ring(k) for k in (0, 3, 1, 2)}
+    r_full = Ring(lambda v: full.at[rows_of(4 * c + v)], "x", (pl.ds(0, 48),), (pl.ds(48, 40),))
 
     r_na.start()
     r_ca.start()
-
-    def stage_clean(i, carry):
-        cols = pl.ds(pl.multiple_of(i * LANES, LANES), LANES)
-        cg[z, :, cols] = jnp.concatenate([masked(0, cols), pad], axis=0).astype(BF16)
-        return carry
-
-    lax.fori_loop(0, (WA + WB) // LANES, stage_clean, 0)
+    r_ay.start()
     r_cg.start()
-
-    def stage_a(i, carry):
-        cols = pl.ds(pl.multiple_of(i * LANES, LANES), LANES)
-        ga[z, y, :, cols] = jnp.concatenate([masked(1, cols), masked(2, cols)], axis=0).astype(BF16)
-        return carry
-
-    lax.fori_loop(0, WA // LANES, stage_a, 0)
-    r_ay.start()
-
-    def stage_b(i, carry):
-        cols = pl.ds(pl.multiple_of(i * LANES, LANES), LANES)
-        from_cols = pl.ds(pl.multiple_of(WA + i * LANES, LANES), LANES)
-        gb[y, z, :, cols] = jnp.concatenate(
-            [masked(1, from_cols), masked(2, from_cols)], axis=0).astype(BF16)
-        return carry
-
-    lax.fori_loop(0, WB // LANES, stage_b, 0)
     r_bz.start()
+
+    r_na.forward()
     r_by[0].start()
-    r_az[0].start()
-
-    r_na.forward()
     here = pl.ds(2 * c, 2)
     there = pl.ds(2 * (1 - c), 2)
     for i, ((zs, ys), same) in enumerate(zip(sources, source_self)):
@@ -210,15 +215,28 @@
 
     r_ca.forward()
     r_cg.forward()
+    r_az[0].start()
     r_ay.forward()
     r_az[3].start()
     r_az[1].start()
     r_bz.forward()
+
+    contract = (((1,), (1,)), ((), ()))
+
+    def gram(left, right):
+        return lax.dot_general(left, right, contract, preferred_element_type=F32)
+
+    r_na.finish()
+    r_ca.finish()
+    part_gram[...] = gram(na[...].reshape(4 * NOISE, 1024), ca[...].reshape(4 * CLEAN_ROWS, 1024))
+    own_half = pl.ds(pl.multiple_of(c * 352, 8), 352)
+    other_half = pl.ds(pl.multiple_of((1 - c) * 352, 8), 352)
+    swap = copy(part_gram.at[other_half], d2, d_s.at[0], d_r.at[0], partner)
+    swap.start()
+
+    r_by[0].forward()
     r_by[3].start()
     r_by[1].start()
-    r_by[0].forward()
-    r_az[0].forward()
-
     for r in range(1, 4):
         block = ao.at[mod4(x + 4 - r), here]
         copy(block, block, x_s.at[r - 1], x_r.at[r - 1], partner).wait_recv()
@@ -226,25 +244,70 @@
         relay.start()
         core.append(relay)
 
-    contract = (((1,), (1,)), ((), ()))
-
-    def gram(left, right):
-        return lax.dot_general(left, right, contract, preferred_element_type=F32)
-
-    r_na.finish()
-    r_ca.finish()
-    gr[0] = gram(na[...].reshape(4 * NOISE, 1024), ca[...].reshape(4 * CLEAN_ROWS, 1024))
+    swap.wait_recv()
+    sm[...] = part_gram[own_half] + d2[...]
+    up, down, across = mod4(x + 1), mod4(x + 3), mod4(x + 2)
+    dev_up, dev_down = (z, y, 2 * up + c), (z, y, 2 * down + c)
+    first = pl.ds(pl.multiple_of(across * SEG, 8), 48)
+    second = pl.ds(pl.multiple_of(across * SEG + 48, 8), 40)
+    share = [copy(sm.at[first], near_a, m_s.at[0], m_r.at[0], dev_up),
+             copy(sm.at[second], near_b, m_s.at[1], m_r.at[1], dev_down),
+             copy(sm.at[rows_of(up)], x3.at[0], m_s.at[2], m_r.at[2], dev_up),
+             copy(sm.at[rows_of(down)], x3.at[1], m_s.at[3], m_r.at[3], dev_down)]
+    share[0].start()
+    share[1].start()
+    r_az[0].forward()
+    share[0].wait_recv()
+    sm[pl.ds(pl.multiple_of(up * SEG, 8), 48)] += near_a[...]
+    share[2].start()
+    share[1].wait_recv()
+    sm[pl.ds(pl.multiple_of(down * SEG + 48, 8), 40)] += near_b[...]
+    share[3].start()
+
     r_cg.finish()
     r_ay.finish()
     r_az[2].start()
+    grad_gram[...] = gram(ga[z].reshape(4 * NOISE, WA), cg[:, :, :WA].reshape(4 * CLEAN_ROWS, WA))
+
+    share[2].wait_recv()
+    share[3].wait_recv()
+    full[rows_of(4 * c + x)] = sm[rows_of(x)] + x3[0] + x3[1]
+    r_full.start()
     r_bz.finish()
     r_by[2].start()
+    r_full.forward()
+    r_full.finish()
+    give = copy(full.at[own_half], full.at[own_half], d_s.at[1], d_r.at[1], partner)
+    give.start()
+
     r_by[0].finish()
-    gr[1] = gram(ga[z].reshape(4 * NOISE, WA), cg[:, :, :WA].reshape(4 * CLEAN_ROWS, WA)) + gram(
-        gb[:, z].reshape(4 * NOISE, WB), cg[:, :, WA:].reshape(4 * CLEAN_ROWS, WB))
-    away = gr.at[:, pl.ds(pl.multiple_of((1 - c) * 352, 8), 352)]
-    swap = copy(away, d2, d_s, d_r, partner)
-    swap.start()
+    grad_gram[...] += gram(gb[:, z].reshape(4 * NOISE, WB), cg[:, :, WA:].reshape(4 * CLEAN_ROWS, WB))
+    copy(full.at[other_half], full.at[other_half], d_s.at[1], d_r.at[1], partner).wait_recv()
+
+    def row_dot(j):
+        terms = [grad_gram[g * SEG:(g + 1) * SEG] * full[g * SEG:(g + 1) * SEG] for g in range(j, 8, 2)]
+        rows_sum = jnp.sum(terms[0] + terms[1] + terms[2] + terms[3], axis=0, keepdims=True)
+        return jnp.broadcast_to(jnp.sum(rows_sum, axis=1, keepdims=True), (8, LANES))
+
+    place = lax.broadcasted_iota(jnp.int32, (8, LANES), 0)
+    tile = jnp.where(place == 2 * z, row_dot(0), jnp.where(place == 2 * z + 1, row_dot(1), 0.0))
+
+    sends = []
+
+    def send_tile(buf, value, me, n, dev, base):
+        buf[me] = value
+        for r in range(1, n):
+            out = copy(buf.at[me], buf.at[me], v_s.at[base + r], v_r.at[base + r], dev(r))
+            out.start()
+            sends.append(out)
+
+    def sum_tiles(buf, me, n, base):
+        for r in range(1, n):
+            origin = buf.at[lax.rem(me + n - r, n)]
+            copy(origin, origin, v_s.at[base + r], v_r.at[base + r], partner).wait_recv()
+        return jnp.sum(buf[...], axis=0)
+
+    send_tile(sv1, tile, t, 8, lambda r: (z, y, lax.rem(t + r, 8)), 0)
 
     for r in range(4):
         block = ao.at[mod4(x + 4 - r), there]
@@ -259,45 +322,12 @@
 
     lax.fori_loop(0, 4, turn, 0)
 
-    swap.wait_recv()
-    sm[...] = gr[:, pl.ds(pl.multiple_of(c * 352, 8), 352)] + d2[...]
-    share = []
-    for r in range(1, 4):
-        to = mod4(x + r)
-        share.append(copy(sm.at[:, pl.ds(pl.multiple_of(to * SEG, 8), SEG)], x3.at[r - 1],
-                          m_s.at[r - 1], m_r.at[r - 1], (z, y, 2 * to + c)))
-    for k in share:
-        k.start()
-
+    tile = sum_tiles(sv1, t, 8, 0)
+    send_tile(sv2, tile, 4 * z + y, 16, cell, 8)
     for k in (3, 1):
         r_az[k].forward()
         r_by[k].forward()
-
-    for k in share:
-        k.wait_recv()
-    total = sm[:, pl.ds(pl.multiple_of(x * SEG, 8), SEG)] + x3[0] + x3[1] + x3[2]
-    dot = jnp.sum(jnp.sum(total[0] * total[1], axis=0, keepdims=True), axis=1, keepdims=True)
-    slot = 2 * z + lax.rem(x, 2)
-    place = lax.broadcasted_iota(jnp.int32, (8, LANES), 0)
-    tile = jnp.where(place == slot, jnp.broadcast_to(dot, (8, LANES)), 0.0)
-
-    sends = []
-
-    def exchange(buf, value, me, n, dev, base):
-        buf[me] = value
-        out = [copy(buf.at[me], buf.at[me], v_s.at[base + r], v_r.at[base + r], dev(lax.rem(me + r, n)))
-               for r in range(1, n)]
-        for k in out:
-            k.start()
-        sends.extend(out)
-        for r in range(1, n):
-            origin = lax.rem(me + n - r, n)
-            copy(buf.at[origin], buf.at[origin], v_s.at[base + r], v_r.at[base + r], dev(origin)).wait_recv()
-        return jnp.sum(buf[...], axis=0)
-
-    tile = exchange(sv1, tile, t, 8, lambda v: (z, y, v), 0)
-    tile = exchange(sv2, tile, y, 4, lambda v: (z, v, t), 8)
-    tile = exchange(sv3, tile, z, 4, lambda v: (v, y, t), 12)
+    tile = sum_tiles(sv2, 4 * z + y, 16, 8)
     weights = jnp.maximum(-tile, 0.0) / jnp.sum(jnp.abs(tile), axis=0, keepdims=True)
     wts[...] = weights
     for k in range(4):
@@ -305,9 +335,6 @@
         scale[k, SEG:] = jnp.broadcast_to(wts[2 * k + 1:2 * k + 2, :], (SEG, LANES))
     lane = lax.broadcasted_iota(jnp.int32, (1, LANES), 1)
     wout_ref[...] = jnp.where(lane == 0, wts[pl.ds(2 * z, 1), :], wts[pl.ds(2 * z + 1, 1), :])[:, :2]
-
-    r_az[2].forward()
-    r_by[2].forward()
 
     def scaled(raw, s):
         full = jnp.concatenate([s, s], axis=1)
@@ -337,6 +364,8 @@
 
     add_a(0, True)
     add_b(0, True)
+    r_az[2].forward()
+    r_by[2].forward()
     for k in (3, 1):
         add_a(k)
         add_b(k)
@@ -357,7 +386,7 @@
             far_copy.wait_send()
     for ring in rings:
         ring.drain()
-    for k in spread + core + [swap] + share + sends:
+    for k in spread + core + [swap, give] + share + sends:
         k.wait_send()
     out_a.wait()
     out_b.wait()
@@ -381,22 +410,25 @@
             vmem((4, 512, 4 * NOISE), BF16),
             vmem((4, 512, 4 * NOISE), BF16),
             vmem((512, WA + WB), F32),
-            vmem((2, 4 * NOISE, 4 * CLEAN_ROWS), F32),
-            vmem((2, 2 * NOISE, 4 * CLEAN_ROWS), F32),
-            vmem((2, 2 * NOISE, 4 * CLEAN_ROWS), F32),
-            vmem((3, 2, SEG, 4 * CLEAN_ROWS), F32),
+            vmem((4 * NOISE, 4 * CLEAN_ROWS), F32),
+            vmem((4 * NOISE, 4 * CLEAN_ROWS), F32),
+            vmem((4 * NOISE, 4 * CLEAN_ROWS), F32),
+            vmem((2 * NOISE, 4 * CLEAN_ROWS), F32),
+            vmem((2 * NOISE, 4 * CLEAN_ROWS), F32),
+            vmem((48, 4 * CLEAN_ROWS), F32),
+            vmem((40, 4 * CLEAN_ROWS), F32),
+            vmem((2, SEG, 4 * CLEAN_ROWS), F32),
             vmem((8, 8, LANES), F32),
-            vmem((4, 8, LANES), F32),
-            vmem((4, 8, LANES), F32),
+            vmem((16, 8, LANES), F32),
             vmem((8, LANES), F32),
             vmem((4, NOISE, LANES), F32),
-            dma((13, 4)), dma((13, 4)),
+            dma((14, 4)), dma((14, 4)),
             dma((8,)), dma((8,)), dma,
             dma((3,)), dma((3,)),
             dma((4,)), dma((4,)),
-            dma, dma,
-            dma((3,)), dma((3,)),
-            dma((16,)), dma((16,)),
+            dma((2,)), dma((2,)),
+            dma((4,)), dma((4,)),
+            dma((24,)), dma((24,)),
             dma((2,)),
         ],
         compiler_params=pltpu.CompilerParams(

time: 112 us -> 96.6 us (0.86)
  Pallas kernels: 106 us -> 90.7 us
    pallas_call x1, Pallas kernels: 106 us -> 90.7 us  [body(): pl.pallas_call(body_kernel, out_shape=(jax.ShapeDtypeStruct((512, WA + WB...]
where the time goes in v1:
time: 96.6 us; the launch traced here: 96 us
  Pallas kernels  90.7 us (94%)
  local copies, waits for them, and re-layouts  4.63 us (5%)
    pallas_call x1, Pallas kernels, body(): pl.pallas_call(body_kernel, out_shape=(jax.ShapeDtypeStruct((512, WA + WB...  90.7 us
    unnamed x4, local copies, waits for them, and re-layouts  4.63 us

profile of v1, /device:TPU:0, one launch (start us, length us, event | category | flops | bytes accessed | tf_op | source)
XLA Modules:
  0.0 96.0 jit_solution(13239779243853651121)
XLA Ops:
  0.6 90.7 %reweight.1 = (f32[512,1792]{1,0:T(8,128)}, f32[1,2]{1,0:T(1,128)}) custom-call(s32[1,3]{1,0:T(1,128)} %ids_ref.1, s32[1,3]{1,0:T(1,128)} %counts_ref.1, bf16[3,88,1024]{2,1,0:T(8,128)(2,1)} %acts_ref.1, bf16[3,88,1792]{2,1,0:T(8,128)(2,1)} %cot_ref.1), custom_call_target="tpu_custom_call" | custom-call | flops 8000000000 | bytes 8000000 | tf_op jit(solution)/shard_map/reweight/pallas_call | solution.py:398
  91.4 0.0 copy-start
  91.4 4.1 %copy.8 = f32[512,1792]{1,0:T(8,128)} copy(f32[512,1792]{1,0:T(8,128)} %get-tuple-element.4) | data formatting | bytes 7340032
  95.5 0.0 copy-done
  95.5 0.5 copy.9
Async XLA Ops:
  91.4 4.1 %copy-start = (f32[1,2]{1,0:T(1,128)S(1)}, f32[1,2]{1,0:T(1,128)}, u32[]{:S(2)}) copy-start(f32[1,2]{1,0:T(1,128)} %get-tuple-element.5) | copy-start | bytes 28
